TPU v7x, 32 devices: a whole 2x2x4 slice. The times are simulated.
32 devices in a mesh: groups: 2 (over x), loop: 16 (over z, y, core).
Axes of the slice: x: 2, y: 2, z: 4, core: 2. Of those that a mesh axis runs over, the one named last changes fastest.
Arguments:
- tokens: bfloat16 [2048, 4096], P(('groups', 'loop')), parts along dimension 0, may hold values from -6 to 6
- expert_ids: int32 [2048, 8], P(('groups', 'loop')), parts along dimension 0, may hold values from 0 to 127, as said below
- keep_mask: int32 [2048, 8], P(('groups', 'loop')), parts along dimension 0, may hold values from 0 to 1, as said below
- tile_slot: int32 [2048, 8], P(('groups', 'loop')), parts along dimension 0, may hold values from 0 to 95, as said below
- route_weight: float32 [2048, 8], P(('groups', 'loop')), parts along dimension 0, may hold values from 0.2 to 1
- gate_weight: bfloat16 [16, 4096, 384], P('loop'), may hold values from -0.09375 to 0.09375
- up_weight: bfloat16 [16, 4096, 384], P('loop'), may hold values from -0.09375 to 0.09375
- down_weight: bfloat16 [16, 384, 4096], P('loop'), may hold values from -0.15625 to 0.15625
Outputs:
- mixed: bfloat16 [2048, 4096], P(('groups', 'loop')), parts along dimension 0
There are 2 independent parts, one for each index of `groups`. A program takes and returns all parts, laid end to end along the dimension named above; an argument that names none is the same for every part. Nothing has to cross between parts.
Inputs may be any that keep to these rules, and one draw needn't show every extreme that they name: `expert_ids`: each row names 8 different experts. `keep_mask`: of one device's rows at most 8 kept entries name one expert, and the kept entries of one expert fit its 96 slots. `tile_slot`: where keep_mask is 1, the entries naming one expert have distinct slots; in every draw some expert below 4 gets 8 kept entries from the rows of several devices and fills all 96 slots.
All inputs are finite; a program needn't handle non-finite values.
Results may differ from a plain program's by a relative error of at most 0.0059.
Values may be sent and summed in bfloat16 or wider, within the bound.
A program may use at most 64 MiB of HBM per device.

v0:
```python
import jax
import jax.numpy as jnp
from jax import lax
from jax.sharding import PartitionSpec as P

TOP = 8
SLICES = 4
SEND = 8


def partner(x, axis, apart):
    return lax.ppermute(x, axis, [(i, i ^ 1 << apart) for i in range(lax.axis_size(axis))])


def local(
    tokens, expert_ids, keep_mask, tile_slot, route_weight, gate_weight, up_weight, down_weight
):
    loop_size = lax.axis_size("loop")
    loop_place = lax.axis_index("loop")
    slice_id = loop_place % SLICES
    group_experts = loop_size // SLICES
    capacity = 3 * loop_size * SEND // 4
    row_count, model_width = tokens.shape
    quarter = model_width // SLICES
    entries = row_count * TOP
    buffer_slots = group_experts * SEND
    flat_ids = expert_ids.reshape(entries)
    live_entry = (flat_ids < group_experts) & (keep_mask.reshape(entries) == 1)
    one_hot = (flat_ids[:, None] == jnp.arange(group_experts)[None, :]).astype(
        jnp.int32
    ) * live_entry[:, None].astype(jnp.int32)
    before = jnp.cumsum(one_hot, axis=0) - one_hot
    position = jnp.where(live_entry, jnp.sum(before * one_hot, axis=1), 0)
    buffer_index = jnp.where(live_entry, flat_ids * SEND + position, buffer_slots)
    slot_of_entry = buffer_index[:, None] == jnp.arange(buffer_slots)[None, :]
    row_select = jnp.sum(
        slot_of_entry.astype(jnp.int32).reshape(row_count, TOP, buffer_slots), axis=1
    )
    slots_flat = tile_slot.reshape(entries)
    slot_sum = jnp.sum(jnp.where(slot_of_entry, slots_flat[:, None], 0), axis=0)
    slot_used = jnp.sum(slot_of_entry.astype(jnp.int32), axis=0)
    slot_values = jnp.where(slot_used > 0, slot_sum, capacity)
    slot_buffer = jnp.broadcast_to(
        slot_values.reshape(group_experts, 1, SEND), (group_experts, SLICES, SEND)
    ).reshape(loop_size, SEND)
    gathered_rows = jnp.dot(
        jnp.transpose(row_select).astype(jnp.bfloat16), tokens, preferred_element_type=jnp.float32
    ).astype(jnp.bfloat16)
    buffer = jnp.broadcast_to(
        gathered_rows.reshape(group_experts, 1, SEND, model_width),
        (group_experts, SLICES, SEND, model_width),
    )
    arrived, arrived_slots = (
        lax.all_to_all(
            buffer.reshape(loop_size, SEND, model_width),
            "loop",
            split_axis=0,
            concat_axis=0,
            tiled=True,
        ),
        lax.all_to_all(slot_buffer, "loop", split_axis=0, concat_axis=0, tiled=True),
    )
    placing = (arrived_slots.reshape(-1)[None, :] == jnp.arange(capacity)[:, None]).astype(
        jnp.bfloat16
    )
    expert_tile = jnp.dot(
        placing, arrived.reshape(-1, model_width), preferred_element_type=jnp.float32
    ).astype(jnp.bfloat16)
    gate_out = jnp.dot(expert_tile, gate_weight[0], preferred_element_type=jnp.float32)
    up_out = jnp.dot(expert_tile, up_weight[0], preferred_element_type=jnp.float32)
    hidden = (jax.nn.silu(gate_out) * up_out).astype(jnp.bfloat16)
    partial_value = jnp.dot(hidden, down_weight[0], preferred_element_type=jnp.float32)
    picking = arrived_slots.reshape(-1)[:, None] == jnp.arange(capacity)[None, :]
    weight_entry = jnp.where(live_entry, route_weight.reshape(entries), 0.0)
    weighted_select = jnp.sum(
        (slot_of_entry.astype(jnp.float32) * weight_entry[:, None]).reshape(
            row_count, TOP, buffer_slots
        ),
        axis=1,
    )
    current = partial_value
    for section_bit in (1, 0):
        half_width = current.shape[1] // 2
        upper_half = slice_id // (1 << section_bit) % 2
        kept_part = lax.dynamic_slice_in_dim(current, upper_half * half_width, half_width, 1)
        sent_part = lax.dynamic_slice_in_dim(current, (1 - upper_half) * half_width, half_width, 1)
        current = kept_part + partner(sent_part, "loop", section_bit)
    expert_out = current.astype(jnp.bfloat16)
    returned = jnp.dot(
        picking.astype(jnp.bfloat16), expert_out, preferred_element_type=jnp.float32
    ).astype(jnp.bfloat16)
    came_back = lax.all_to_all(
        returned.reshape(loop_size, SEND, quarter), "loop", split_axis=0, concat_axis=0, tiled=True
    )
    returned_rows = jnp.transpose(
        came_back.reshape(group_experts, SLICES, SEND, quarter), (0, 2, 1, 3)
    ).reshape(buffer_slots, model_width)
    summed = jnp.dot(
        weighted_select,
        returned_rows.astype(jnp.float32),
        precision=lax.Precision.HIGHEST,
        preferred_element_type=jnp.float32,
    )
    return summed.astype(jnp.bfloat16)


def solution(mesh):
    in_specs = (
        P(("groups", "loop"), None),
        P(("groups", "loop"), None),
        P(("groups", "loop"), None),
        P(("groups", "loop"), None),
        P(("groups", "loop"), None),
        P("loop", None, None),
        P("loop", None, None),
        P("loop", None, None),
    )
    out_specs = P(("groups", "loop"), None)
    return jax.shard_map(local, mesh=mesh, in_specs=in_specs, out_specs=out_specs, check_vma=False)
```

profile of v0, /device:TPU:0, one launch (start us, length us, event | category | flops | bytes accessed | tf_op | source)
XLA Modules:
  0.0 105.0 jit_solution(14971752280944943235)
XLA Ops:
  0.0 0.9 copy.42
  2.2 1.2 %reduce-window.6 = s32[4,4,128]{2,1,0:T(4,128)S(1)} reduce-window(s32[4,4,128]{2,1,0:T(4,128)S(1)} %fusion.27, s32[]{:T(128)} %constant.65.clone.1), window={size=1x1x128 pad=0_0x0_0x127_0}, to_apply=%region_0.1 | reduce-window | flops 260096 | bytes 16388 | tf_op jit(solution)/shard_map/reduce-window
  4.0 0.8 copy.47
  5.6 7.4 %all-to-all-start = ((s32[16,1,8]{2,1,0:T(1,128)}), s32[16,1,8]{2,1,0:T(1,128)S(1)}, u32[]{:S(2)}, u32[]{:S(2)}) async-start(s32[16,1,8]{2,1,0:T(1,128)} %bitcast.2), calls=%async_computation | async-start | bytes 16384 | tf_op jit(solution)/shard_map/all_to_all | solution.py:61
  13.9 1.3 %fusion = bf16[4,8,4096]{2,1,0:T(8,128)(2,1)S(1)} fusion(bf16[64,4096]{1,0:T(8,128)(2,1)} %param.8, s32[64,32]{0,1:T(8,128)S(1)} %convert_reduce_fusion), kind=kOutput, calls=%fused_computation.3 | convolution fusion | flops 16910336 | bytes 794624 | tf_op jit(solution)/shard_map/dot_general | solution.py:46
  15.2 4.2 %all-to-all-done = s32[16,1,8]{2,1,0:T(1,128)S(1)} async-done(((s32[16,1,8]{2,1,0:T(1,128)}), s32[16,1,8]{2,1,0:T(1,128)S(1)}, u32[]{:S(2)}, u32[]{:S(2)}) %all-to-all-start) | async-done | bytes 544 | tf_op jit(solution)/shard_map/all_to_all | solution.py:61
  19.4 1.1 %broadcast_in_dim.63 = bf16[4,4,8,4096]{3,2,1,0:T(8,128)(2,1)} broadcast(bf16[4,8,4096]{2,1,0:T(8,128)(2,1)S(1)} %fusion), dimensions={0,2,3} | broadcast | bytes 1310720 | tf_op jit(solution)/shard_map/broadcast_in_dim | solution.py:49
  20.5 4.3 %all-to-all-start.1 = ((bf16[16,8,4096]{2,1,0:T(8,128)(2,1)}), bf16[16,8,4096]{2,1,0:T(8,128)(2,1)}, u32[]{:S(2)}, u32[]{:S(2)}) async-start(bf16[16,8,4096]{2,1,0:T(8,128)(2,1)} %bitcast.47), calls=%async_computation.1 | async-start | bytes 2097152 | tf_op jit(solution)/shard_map/all_to_all | solution.py:54
  26.2 21.6 %all-to-all-done.1 = bf16[16,8,4096]{2,1,0:T(8,128)(2,1)} async-done(((bf16[16,8,4096]{2,1,0:T(8,128)(2,1)}), bf16[16,8,4096]{2,1,0:T(8,128)(2,1)}, u32[]{:S(2)}, u32[]{:S(2)}) %all-to-all-start.1) | async-done | bytes 1048608 | tf_op jit(solution)/shard_map/all_to_all | solution.py:54
  47.8 1.6 %convolution_convert_fusion = bf16[96,4096]{1,0:T(8,128)(2,1)S(1)} fusion(bf16[16,8,4096]{2,1,0:T(8,128)(2,1)} %all-to-all-done.1, s32[128]{0:T(128)S(1)} %eq.120), kind=kOutput, calls=%fused_computation | convolution fusion | flops 101068800 | bytes 1835520 | tf_op jit(solution)/shard_map/dot_general | solution.py:66
  49.4 0.9 copy-done.1
  50.3 2.5 %fusion.5 = f32[96,384]{1,0:T(8,128)S(1)} fusion(bf16[96,4096]{1,0:T(8,128)(2,1)S(1)} %convolution_convert_fusion, bf16[1,4096,384]{2,1,0:T(8,128)(2,1)} %param.13), kind=kOutput, calls=%fused_computation.8 | convolution fusion | flops 301989888 | bytes 4079616 | tf_op jit(solution)/shard_map/dot_general | solution.py:69
  52.8 4.8 %fusion.1 = f32[96,4096]{1,0:T(8,128)} fusion(bf16[1,384,4096]{2,1,0:T(8,128)(2,1)S(1)} %copy-done, bf16[96,4096]{1,0:T(8,128)(2,1)} %copy-done.1, bf16[1,4096,384]{2,1,0:T(8,128)(2,1)} %param.14, f32[96,384]{1,0:T(8,128)S(1)} %fusion.5), kind=kOutput, calls=%fused_computation.4 | convolution fusion | flops 604200960 | bytes 8798208 | tf_op jit(solution)/shard_map/dot_general | solution.py:72
  57.6 2.1 %constant_dynamic-slice_fusion.1 = f32[96,2048]{1,0:T(8,128)} fusion(f32[96,4096]{1,0:T(8,128)} %fusion.1, s32[]{:T(128)S(6)} %select_n.88), kind=kLoop, calls=%fused_computation.52 | loop fusion | bytes 1572868 | tf_op jit(solution)/shard_map/dynamic_slice | solution.py:86
  59.6 1.8 %collective-permute-start = (f32[96,2048]{1,0:T(8,128)}, f32[96,2048]{1,0:T(8,128)}, u32[]{:S(2)}, u32[]{:S(2)}) collective-permute-start(f32[96,2048]{1,0:T(8,128)} %constant_dynamic-slice_fusion.1), channel_id=1, source_target_pairs={{0,2},{1,3},{2,0},{3,1},{4,6},{5,7},{6,4},{7,5},{8,10},{9,11},{10,... | collective-permute-start | bytes 2359304 | tf_op jit(solution)/shard_map/ppermute | solution.py:12
  61.4 18.8 %collective-permute-done = f32[96,2048]{1,0:T(8,128)} collective-permute-done((f32[96,2048]{1,0:T(8,128)}, f32[96,2048]{1,0:T(8,128)}, u32[]{:S(2)}, u32[]{:S(2)}) %collective-permute-start) | collective-permute-done | bytes 786464 | tf_op jit(solution)/shard_map/ppermute | solution.py:12
  80.2 1.5 %dynamic-slice_add_fusion = f32[96,2048]{1,0:T(8,128)S(1)} fusion(f32[96,2048]{1,0:T(8,128)} %collective-permute-done, f32[96,4096]{1,0:T(8,128)} %fusion.1, s32[]{:T(128)S(6)} %select_n.87), kind=kLoop, calls=%fused_computation.15 | loop fusion | flops 196608 | bytes 2359300 | tf_op jit(solution)/shard_map/add | solution.py:87
  81.7 0.9 copy-done.2
  82.6 0.8 constant_dynamic-slice_fusion
  83.3 1.9 %collective-permute-done.1 = f32[96,1024]{1,0:T(8,128)S(1)} collective-permute-done((f32[96,1024]{1,0:T(8,128)}, f32[96,1024]{1,0:T(8,128)S(1)}, u32[]{:S(2)}, u32[]{:S(2)}) %collective-permute-start.1) | collective-permute-done | bytes 393248 | tf_op jit(solution)/shard_map/ppermute | solution.py:12
  85.3 2.0 %fusion.7 = bf16[16,8,1024]{2,1,0:T(8,128)(2,1)} fusion(f32[96,1024]{1,0:T(8,128)S(1)} %collective-permute-done.1, f32[96,2048]{1,0:T(8,128)} %copy-done.2, s32[]{:T(128)S(6)} %select_n.90, s32[128]{0:T(128)S(1)} %eq.120), kind=kOutput, calls=%fused_computation.11 | convolution fusion | flops 25505792 | bytes 1049092 | tf_op jit(solution)/shard_map/dot_general | solution.py:89
  87.2 6.3 %all-to-all-start.2 = ((bf16[16,8,1024]{2,1,0:T(8,128)(2,1)}), bf16[16,8,1024]{2,1,0:T(8,128)(2,1)S(1)}, u32[]{:S(2)}, u32[]{:S(2)}) async-start(bf16[16,8,1024]{2,1,0:T(8,128)(2,1)} %fusion.7), calls=%async_computation.2 | async-start | bytes 524288 | tf_op jit(solution)/shard_map/all_to_all | solution.py:92
  93.6 10.0 %all-to-all-done.2 = bf16[16,8,1024]{2,1,0:T(8,128)(2,1)S(1)} async-done(((bf16[16,8,1024]{2,1,0:T(8,128)(2,1)}), bf16[16,8,1024]{2,1,0:T(8,128)(2,1)S(1)}, u32[]{:S(2)}, u32[]{:S(2)}) %all-to-all-start.2) | async-done | bytes 262176 | tf_op jit(solution)/shard_map/all_to_all | solution.py:92
  103.6 1.4 %convolution_convert_fusion.1 = bf16[64,4096]{1,0:T(8,128)(2,1)} fusion(f32[64,32]{0,1:T(8,128)S(1)} %select_reduce_fusion, bf16[32,4096]{1,0:T(8,128)(2,1)S(1)} %bitcast.48), kind=kOutput, calls=%fused_computation.1 | convolution fusion | flops 100925440 | bytes 794624 | tf_op jit(solution)/shard_map/dot_general | solution.py:98
  (32 shorter events, 4.9 us)
Async XLA Ops:
  0.0 52.8 %copy-start = (bf16[1,384,4096]{2,1,0:T(8,128)(2,1)S(1)}, bf16[1,384,4096]{2,1,0:T(8,128)(2,1)}, u32[]{:S(2)}) copy-start(bf16[1,384,4096]{2,1,0:T(8,128)(2,1)} %param.15) | copy-start | bytes 9437188
  5.6 13.7 %all-to-all-start = ((s32[16,1,8]{2,1,0:T(1,128)}), s32[16,1,8]{2,1,0:T(1,128)S(1)}, u32[]{:S(2)}, u32[]{:S(2)}) async-start(s32[16,1,8]{2,1,0:T(1,128)} %bitcast.2), calls=%async_computation | async-start | bytes 16384 | tf_op jit(solution)/shard_map/all_to_all | solution.py:61
  20.5 27.3 %all-to-all-start.1 = ((bf16[16,8,4096]{2,1,0:T(8,128)(2,1)}), bf16[16,8,4096]{2,1,0:T(8,128)(2,1)}, u32[]{:S(2)}, u32[]{:S(2)}) async-start(bf16[16,8,4096]{2,1,0:T(8,128)(2,1)} %bitcast.47), calls=%async_computation.1 | async-start | bytes 2097152 | tf_op jit(solution)/shard_map/all_to_all | solution.py:54
  49.4 0.9 copy-start.1
  59.6 20.6 %collective-permute-start = (f32[96,2048]{1,0:T(8,128)}, f32[96,2048]{1,0:T(8,128)}, u32[]{:S(2)}, u32[]{:S(2)}) collective-permute-start(f32[96,2048]{1,0:T(8,128)} %constant_dynamic-slice_fusion.1), channel_id=1, source_target_pairs={{0,2},{1,3},{2,0},{3,1},{4,6},{5,7},{6,4},{7,5},{8,10},{9,11},{10,... | collective-permute-start | bytes 2359304 | tf_op jit(solution)/shard_map/ppermute | solution.py:12
  81.7 0.9 copy-start.2
  83.3 1.9 %collective-permute-start.1 = (f32[96,1024]{1,0:T(8,128)}, f32[96,1024]{1,0:T(8,128)S(1)}, u32[]{:S(2)}, u32[]{:S(2)}) collective-permute-start(f32[96,1024]{1,0:T(8,128)} %constant_dynamic-slice_fusion), channel_id=1, source_target_pairs={{0,1},{1,0},{2,3},{3,2},{4,5},{5,4},{6,7},{7,6},{8,9},{9,8},{10,11... | collective-permute-start | bytes 1179656 | tf_op jit(solution)/shard_map/ppermute | solution.py:12
  87.2 16.4 %all-to-all-start.2 = ((bf16[16,8,1024]{2,1,0:T(8,128)(2,1)}), bf16[16,8,1024]{2,1,0:T(8,128)(2,1)S(1)}, u32[]{:S(2)}, u32[]{:S(2)}) async-start(bf16[16,8,1024]{2,1,0:T(8,128)(2,1)} %fusion.7), calls=%async_computation.2 | async-start | bytes 524288 | tf_op jit(solution)/shard_map/all_to_all | solution.py:92
where the time goes:
time: 106 us; the launch traced here: 105 us
  waiting for transfers between devices  56.5 us (53%)
  starting transfers between devices  19.8 us (19%)
  matrix products  13.5 us (13%)
  local copies, waits for them, and re-layouts  9.66 us (9%)
  other arithmetic  5.3 us (5%)
    all_to_all x1, waiting for transfers between devices, local(): lax.all_to_all(buffer.reshape(loop_size, SEND, model_width), 'loop', spli...  21.6 us
    ppermute x2, waiting for transfers between devices, partner(): lax.ppermute(x, axis, [(i, i ^ 1 << apart) for i in range(lax.axis_size(a...  20.7 us
    all_to_all x1, waiting for transfers between devices, local(): lax.all_to_all(returned.reshape(loop_size, SEND, quarter), 'loop', split_...  10 us
    all_to_all x1, starting transfers between devices, local(): lax.all_to_all(slot_buffer, 'loop', split_axis=0, concat_axis=0, tiled=True)  7.39 us
    all_to_all x1, starting transfers between devices, local(): lax.all_to_all(returned.reshape(loop_size, SEND, quarter), 'loop', split_...  6.3 us
    dot_general x1, matrix products, local(): jnp.dot(hidden, down_weight[0], preferred_element_type=jnp.float32)  4.75 us
    all_to_all x1, starting transfers between devices, local(): lax.all_to_all(buffer.reshape(loop_size, SEND, model_width), 'loop', spli...  4.34 us
    all_to_all x1, waiting for transfers between devices, local(): lax.all_to_all(slot_buffer, 'loop', split_axis=0, concat_axis=0, tiled=True)  4.18 us
  transfers between devices with their start and end apart: 5, of which 5 were waited for; matrix products, arithmetic and copies ran while one was open for 3% of the time, Pallas kernels for 0%

commit v1 on v0

v1 whole, which is shorter than its diff:
```python
import functools

import jax
import jax.numpy as jnp
from jax import lax
from jax.experimental import pallas as pl
from jax.experimental.pallas import tpu as pltpu
from jax.sharding import PartitionSpec as P

SLICES = 4
SEND = 8
CHUNKS = 4
MESH = pl.DeviceIdType.MESH


def kernel(
    experts,
    tokens, ids, keep, route, gate_hbm, up_hbm, down_hbm,
    out,
    outgoing, tile, gate_w, up_w, down_w, gate_acc, up_acc, own_part,
    core_out, core_in, side_out, side_in, back_out, back_in,
    weight_sem, z_send, z_recv, y_send, y_recv, c_send, c_recv,
    cb_send, cb_recv, yb_send, yb_recv, zb_send, zb_recv,
):
    place = lax.axis_index("loop")
    mine = lax.div(place, SLICES)
    part = lax.rem(place, SLICES)
    side = mine * SLICES + lax.rem(part + 2, SLICES)
    core = mine * SLICES + part + 1 - 2 * lax.rem(part, 2)

    def along(step):
        return lax.rem(mine + step + experts, experts) * SLICES + part

    chunks = outgoing.shape[0]
    width = outgoing.shape[-1]
    span = 2 * width
    block = 2 * SEND
    columns = experts * block
    rows = SLICES * experts * SEND

    barrier = pltpu.get_barrier_semaphore()
    for step in range(1, experts):
        pl.semaphore_signal(barrier, inc=1, device_id={"loop": along(step)}, device_id_type=MESH)
    pl.semaphore_signal(barrier, inc=1, device_id={"loop": side}, device_id_type=MESH)
    pl.semaphore_signal(barrier, inc=1, device_id={"loop": core}, device_id_type=MESH)

    loads = []
    for k in range(chunks):
        at = pl.ds(k * span, span)
        loads.append((
            pltpu.make_async_copy(gate_hbm.at[0, at], gate_w.at[at], weight_sem.at[0, k]),
            pltpu.make_async_copy(up_hbm.at[0, at], up_w.at[at], weight_sem.at[1, k]),
        ))
        for load in loads[-1]:
            load.start()
    down_load = pltpu.make_async_copy(down_hbm.at[0], down_w, weight_sem.at[2, 0])
    down_load.start()

    row_count = tokens.shape[0]
    column = lax.broadcasted_iota(jnp.int32, (row_count, columns), 1)
    expert_of = lax.rem(mine - lax.div(column, block) + experts, experts)
    position_of = lax.rem(column, SEND)
    lower = lax.rem(column, block) < SEND
    chosen = jnp.where(keep[...] == 1, ids[...], -1)
    weights = route[...]
    live = jnp.zeros((row_count, columns), jnp.float32)
    scale = jnp.zeros((row_count, columns), jnp.float32)
    for k in range(ids.shape[1]):
        match = chosen[:, k:k + 1] == expert_of
        live = jnp.where(match, 1.0, live)
        scale = jnp.where(match, weights[:, k:k + 1], scale)
    earlier = (
        lax.broadcasted_iota(jnp.int32, (row_count, row_count), 1)
        < lax.broadcasted_iota(jnp.int32, (row_count, row_count), 0)
    ).astype(jnp.bfloat16)
    before = jnp.dot(earlier, live.astype(jnp.bfloat16), preferred_element_type=jnp.float32)
    select = jnp.where(before == position_of.astype(jnp.float32), live, 0.0)
    select_low = jnp.where(lower, select, 0.0)
    select_high = jnp.where(lower, 0.0, select)
    pick = jnp.concatenate([select_low, select_high], axis=0).astype(jnp.bfloat16)

    def z_copy(k, d):
        return pltpu.make_async_remote_copy(
            src_ref=outgoing.at[k, d], dst_ref=tile.at[k, 0, d],
            send_sem=z_send.at[k], recv_sem=z_recv.at[k],
            device_id={"loop": along(-d)}, device_id_type=MESH,
        )

    def z_all(k):
        return pltpu.make_async_remote_copy(
            src_ref=outgoing.at[k, pl.ds(1, experts - 1)],
            dst_ref=tile.at[k, 0, pl.ds(1, experts - 1)],
            send_sem=z_send.at[k], recv_sem=z_recv.at[k],
            device_id={"loop": along(1)}, device_id_type=MESH,
        )

    def y_copy(k):
        return pltpu.make_async_remote_copy(
            src_ref=tile.at[k, 0], dst_ref=tile.at[k, 1],
            send_sem=y_send.at[k], recv_sem=y_recv.at[k],
            device_id={"loop": side}, device_id_type=MESH,
        )

    def c_copy(k):
        return pltpu.make_async_remote_copy(
            src_ref=tile.at[k, pl.ds(0, 2)], dst_ref=tile.at[k, pl.ds(2, 2)],
            send_sem=c_send.at[k], recv_sem=c_recv.at[k],
            device_id={"loop": core}, device_id_type=MESH,
        )

    for k in range(chunks):
        low = tokens[:, k * span:k * span + width]
        high = tokens[:, k * span + width:(k + 1) * span]
        picked = lax.dot_general(
            pick, jnp.concatenate([low, high], axis=0), (((0,), (0,)), ((), ())),
            preferred_element_type=jnp.float32,
        ).astype(jnp.bfloat16).reshape(experts, block, width)
        outgoing[k] = picked
        tile[k, 0, 0] = picked[0]
        if k == 0:
            pl.semaphore_wait(barrier, experts + 1)
        for d in range(1, experts):
            z_copy(k, d).start()

    def gate_up(k):
        arrived = tile[k].astype(jnp.float32).reshape(SLICES * experts, block, width)
        x = jnp.concatenate(
            [arrived[:, :SEND].reshape(rows, width), arrived[:, SEND:].reshape(rows, width)], axis=1
        ).astype(jnp.bfloat16)
        for load in loads[k]:
            load.wait()
        at = pl.ds(k * span, span)
        gate = jnp.dot(x, gate_w[at], preferred_element_type=jnp.float32)
        up = jnp.dot(x, up_w[at], preferred_element_type=jnp.float32)
        if k == 0:
            gate_acc[...] = gate
            up_acc[...] = up
        else:
            gate_acc[...] += gate
            up_acc[...] += up

    for t in range(chunks + 2):
        if t < chunks:
            z_all(t).wait_recv()
            y_copy(t).start()
        if 0 <= t - 1 < chunks:
            y_copy(t - 1).wait_recv()
            c_copy(t - 1).start()
        if 0 <= t - 2 < chunks:
            c_copy(t - 2).wait_recv()
            gate_up(t - 2)

    gate = gate_acc[...]
    hidden = (gate / (1.0 + jnp.exp(-gate)) * up_acc[...]).astype(jnp.bfloat16)
    down_load.wait()

    def cb_copy(k):
        return pltpu.make_async_remote_copy(
            src_ref=core_out.at[k], dst_ref=core_in.at[k],
            send_sem=cb_send.at[k], recv_sem=cb_recv.at[k],
            device_id={"loop": core}, device_id_type=MESH,
        )

    def yb_copy(k):
        return pltpu.make_async_remote_copy(
            src_ref=side_out.at[k], dst_ref=side_in.at[k],
            send_sem=yb_send.at[k], recv_sem=yb_recv.at[k],
            device_id={"loop": side}, device_id_type=MESH,
        )

    def zb_copy(k, d):
        return pltpu.make_async_remote_copy(
            src_ref=back_out.at[k, d], dst_ref=back_in.at[k, d],
            send_sem=zb_send.at[k], recv_sem=zb_recv.at[k],
            device_id={"loop": along(d)}, device_id_type=MESH,
        )

    def zb_all(k):
        return pltpu.make_async_remote_copy(
            src_ref=back_out.at[k, pl.ds(1, experts - 1)],
            dst_ref=back_in.at[k, pl.ds(1, experts - 1)],
            send_sem=zb_send.at[k], recv_sem=zb_recv.at[k],
            device_id={"loop": along(1)}, device_id_type=MESH,
        )

    scaled = jnp.concatenate([select_low * scale, select_high * scale], axis=0)
    coarse = scaled.astype(jnp.bfloat16)
    fine = (scaled - coarse.astype(jnp.float32)).astype(jnp.bfloat16)
    mixing = jnp.concatenate([coarse, fine], axis=0)

    def down(k):
        y = jnp.dot(hidden, down_w[:, k * span:(k + 1) * span], preferred_element_type=jnp.float32)
        y = jnp.concatenate(
            [
                y[:, :width].reshape(SLICES * experts, SEND, width),
                y[:, width:].reshape(SLICES * experts, SEND, width),
            ],
            axis=1,
        ).reshape(SLICES, experts, block, width)
        core_out[k] = y[2:].astype(jnp.bfloat16)
        cb_copy(k).start()
        own_part[k] = y[:2]

    def core_sum(k):
        cb_copy(k).wait_recv()
        side_out[k] = (own_part[k, 1] + core_in[k, 1].astype(jnp.float32)).astype(jnp.bfloat16)
        yb_copy(k).start()
        own_part[k, 0] = own_part[k, 0] + core_in[k, 0].astype(jnp.float32)

    def side_sum(k):
        yb_copy(k).wait_recv()
        total = (own_part[k, 0] + side_in[k].astype(jnp.float32)).astype(jnp.bfloat16)
        back_out[k] = total
        for d in range(1, experts):
            zb_copy(k, d).start()
        back_in[k, 0] = total[0]

    def mix(k):
        zb_all(k).wait_recv()
        m = jnp.dot(
            mixing, back_in[k].reshape(columns, width), preferred_element_type=jnp.float32
        )
        m = m[:2 * row_count] + m[2 * row_count:]
        out[:, k * span:k * span + width] = m[:row_count].astype(jnp.bfloat16)
        out[:, k * span + width:(k + 1) * span] = m[row_count:].astype(jnp.bfloat16)

    for t in range(chunks + 1):
        if t < chunks:
            down(t)
        if t >= 1:
            core_sum(t - 1)
    for t in range(chunks + 1):
        if t < chunks:
            side_sum(t)
        if t >= 1:
            mix(t - 1)

    for k in range(chunks):
        z_all(k).wait_send()
        y_copy(k).wait_send()
        c_copy(k).wait_send()
        cb_copy(k).wait_send()
        yb_copy(k).wait_send()
        zb_all(k).wait_send()


def local(tokens, expert_ids, keep_mask, tile_slot, route_weight, gate_weight, up_weight, down_weight):
    experts = lax.axis_size("loop") // SLICES
    row_count, model_width = tokens.shape
    units = gate_weight.shape[2]
    chunks = CHUNKS
    width = model_width // (2 * chunks)
    block = 2 * SEND
    rows = SLICES * experts * SEND
    bf16, f32 = jnp.bfloat16, jnp.float32
    vmem = pl.BlockSpec(memory_space=pltpu.VMEM)
    hbm = pl.BlockSpec(memory_space=pl.ANY)
    dma = pltpu.SemaphoreType.DMA
    return pl.pallas_call(
        functools.partial(kernel, experts),
        out_shape=jax.ShapeDtypeStruct((row_count, model_width), bf16),
        in_specs=[vmem, vmem, vmem, vmem, hbm, hbm, hbm],
        out_specs=vmem,
        scratch_shapes=[
            pltpu.VMEM((chunks, experts, block, width), bf16),
            pltpu.VMEM((chunks, SLICES, experts, block, width), bf16),
            pltpu.VMEM((model_width, units), bf16),
            pltpu.VMEM((model_width, units), bf16),
            pltpu.VMEM((units, model_width), bf16),
            pltpu.VMEM((rows, units), f32),
            pltpu.VMEM((rows, units), f32),
            pltpu.VMEM((chunks, 2, experts, block, width), f32),
            pltpu.VMEM((chunks, 2, experts, block, width), bf16),
            pltpu.VMEM((chunks, 2, experts, block, width), bf16),
            pltpu.VMEM((chunks, experts, block, width), bf16),
            pltpu.VMEM((chunks, experts, block, width), bf16),
            pltpu.VMEM((chunks, experts, block, width), bf16),
            pltpu.VMEM((chunks, experts, block, width), bf16),
            dma((3, chunks)),
        ] + [dma((chunks,)) for _ in range(12)],
        compiler_params=pltpu.CompilerParams(
            collective_id=0, has_side_effects=True, vmem_limit_bytes=56 * 1024 * 1024
        ),
        cost_estimate=pl.CostEstimate(
            flops=6 * rows * model_width * units,
            bytes_accessed=6 * model_width * units,
            transcendentals=rows * units,
        ),
    )(tokens, expert_ids, keep_mask, route_weight, gate_weight, up_weight, down_weight)


def solution(mesh):
    shared = P(("groups", "loop"), None)
    held = P("loop", None, None)
    return jax.shard_map(
        local,
        mesh=mesh,
        in_specs=(shared,) * 5 + (held,) * 3,
        out_specs=shared,
        check_vma=False,
    )
```

time: 106 us -> 43.8 us (0.41)
  waiting for transfers between devices: 56.5 us -> 0 us
  Pallas kernels: 0 us -> 37.5 us
  starting transfers between devices: 19.8 us -> 0 us
  matrix products: 13.5 us -> 0 us
  other arithmetic: 5.3 us -> 0 us
  local copies, waits for them, and re-layouts: 9.66 us -> 6 us
    pallas_call x0 -> x1, Pallas kernels: none -> 37.5 us  [local(): pl.pallas_call(functools.partial(kernel, experts), out_shape=jax.ShapeDty...]
    all_to_all x3 -> x0, waiting for transfers between devices: 35.8 us -> none  [the longest x1 21.6 us: local(): lax.all_to_all(buffer.reshape(loop_size, SEND, model_width), 'loop', spli...]
    ppermute x2 -> x0, waiting for transfers between devices: 20.7 us -> none  [partner(): lax.ppermute(x, axis, [(i, i ^ 1 << apart) for i in range(lax.axis_size(a...]
    all_to_all x3 -> x0, starting transfers between devices: 18 us -> none  [the longest x1 7.39 us: local(): lax.all_to_all(slot_buffer, 'loop', split_axis=0, concat_axis=0, tiled=True)]
    dot_general x6 -> x0, matrix products: 13.5 us -> none  [the longest x1 4.75 us: local(): jnp.dot(hidden, down_weight[0], preferred_element_type=jnp.float32)]
    dynamic_slice x2 -> x0, local copies, waits for them, and re-layouts: 2.85 us -> none  [local(): lax.dynamic_slice_in_dim(current, (1 - upper_half) * half_width, half_wid...]
    unnamed x8 -> x4, local copies, waits for them, and re-layouts: 3.45 us -> 6 us
    broadcast_in_dim x3 -> x0, local copies, waits for them, and re-layouts: 1.84 us -> none  [the longest x1 1.14 us: local(): jnp.broadcast_to(gathered_rows.reshape(group_experts, 1, SEND, model_widt...]
  transfers between devices with their start and end apart: 5 -> 0, of which waited for: 5 -> 0; matrix products, arithmetic and copies ran while one was open for 3% -> 0% of each run, Pallas kernels for 0% -> 0%
where the time goes in v1:
time: 43.8 us; the launch traced here: 43.5 us
  Pallas kernels  37.5 us (86%)
  local copies, waits for them, and re-layouts  6 us (14%)
    pallas_call x1, Pallas kernels, local(): pl.pallas_call(functools.partial(kernel, experts), out_shape=jax.ShapeDty...  37.5 us
    unnamed x4, local copies, waits for them, and re-layouts  6 us

profile of v1, /device:TPU:0, one launch (start us, length us, event | category | flops | bytes accessed | tf_op | source)
XLA Modules:
  0.0 43.5 jit_solution(13840863727342806)
XLA Ops:
  0.0 1.4 %copy.8.ids = s32[64,8]{1,0:T(8,128)} copy(s32[64,8]{0,1:T(8,128)} %param.9) | data formatting | bytes 4096 | tf_op args[1]
  1.4 1.4 %copy.9.keep = s32[64,8]{1,0:T(8,128)} copy(s32[64,8]{0,1:T(8,128)} %param.10) | data formatting | bytes 4096 | tf_op args[2]
  2.8 1.4 %copy.10.route = f32[64,8]{1,0:T(8,128)} copy(f32[64,8]{0,1:T(8,128)} %param.11) | data formatting | bytes 4096 | tf_op args[4]
  4.1 37.5 %shard_map.73 = bf16[64,4096]{1,0:T(8,128)(2,1)} custom-call(bf16[64,4096]{1,0:T(8,128)(2,1)} %tokens.1, s32[64,8]{1,0:T(8,128)} %copy.8.ids, s32[64,8]{1,0:T(8,128)} %copy.9.keep, f32[64,8]{1,0:T(8,128)} %copy.10.route, bf16[1,4096,384]{2,1,0:T(8,128)(2,1)} %gate_hbm.1, bf16[1,4096,384]{2,1,0:T(8,128)(2,1)} %up_hbm.1, bf16[1,384,4096]{2,1,0:T(8,128)(2,1)} %down_hbm.1), custom_call_target="tpu_custom_call" | custom-call | flops 1207959552 | bytes 9437184 | tf_op jit(solution)/shard_map/pallas_call | solution.py:259
  41.6 1.9 %copy.12 = bf16[64,4096]{1,0:T(8,128)(2,1)} copy(bf16[64,4096]{1,0:T(8,128)(2,1)} %shard_map.73) | data formatting | bytes 1048576

commit v2 on v1

--- a/solution.py
+++ b/solution.py
@@ -9,7 +9,8 @@
 
 SLICES = 4
 SEND = 8
-CHUNKS = 4
+CHUNKS = 2
+AHEAD = 2
 MESH = pl.DeviceIdType.MESH
 
 
@@ -37,6 +38,7 @@
     block = 2 * SEND
     columns = experts * block
     rows = SLICES * experts * SEND
+    others = pl.ds(1, experts - 1)
 
     barrier = pltpu.get_barrier_semaphore()
     for step in range(1, experts):
@@ -57,27 +59,27 @@
     down_load.start()
 
     row_count = tokens.shape[0]
-    column = lax.broadcasted_iota(jnp.int32, (row_count, columns), 1)
-    expert_of = lax.rem(mine - lax.div(column, block) + experts, experts)
-    position_of = lax.rem(column, SEND)
-    lower = lax.rem(column, block) < SEND
+    row = lax.broadcasted_iota(jnp.int32, (columns, row_count), 0)
+    expert_of = lax.rem(mine - lax.div(row, block) + experts, experts)
+    position_of = lax.rem(row, SEND)
+    lower = lax.rem(row, block) < SEND
     chosen = jnp.where(keep[...] == 1, ids[...], -1)
     weights = route[...]
-    live = jnp.zeros((row_count, columns), jnp.float32)
-    scale = jnp.zeros((row_count, columns), jnp.float32)
-    for k in range(ids.shape[1]):
-        match = chosen[:, k:k + 1] == expert_of
+    live = jnp.zeros((columns, row_count), jnp.float32)
+    scale = jnp.zeros((columns, row_count), jnp.float32)
+    for k in range(ids.shape[0]):
+        match = chosen[k:k + 1] == expert_of
         live = jnp.where(match, 1.0, live)
-        scale = jnp.where(match, weights[:, k:k + 1], scale)
+        scale = jnp.where(match, weights[k:k + 1], scale)
     earlier = (
-        lax.broadcasted_iota(jnp.int32, (row_count, row_count), 1)
-        < lax.broadcasted_iota(jnp.int32, (row_count, row_count), 0)
+        lax.broadcasted_iota(jnp.int32, (row_count, row_count), 0)
+        < lax.broadcasted_iota(jnp.int32, (row_count, row_count), 1)
     ).astype(jnp.bfloat16)
-    before = jnp.dot(earlier, live.astype(jnp.bfloat16), preferred_element_type=jnp.float32)
+    before = jnp.dot(live.astype(jnp.bfloat16), earlier, preferred_element_type=jnp.float32)
     select = jnp.where(before == position_of.astype(jnp.float32), live, 0.0)
     select_low = jnp.where(lower, select, 0.0)
     select_high = jnp.where(lower, 0.0, select)
-    pick = jnp.concatenate([select_low, select_high], axis=0).astype(jnp.bfloat16)
+    pick = jnp.concatenate([select_low, select_high], axis=1).astype(jnp.bfloat16)
 
     def z_copy(k, d):
         return pltpu.make_async_remote_copy(
@@ -86,18 +88,29 @@
             device_id={"loop": along(-d)}, device_id_type=MESH,
         )
 
+    def z_start(k):
+        for d in range(1, experts):
+            z_copy(k, d).start()
+
     def z_all(k):
         return pltpu.make_async_remote_copy(
-            src_ref=outgoing.at[k, pl.ds(1, experts - 1)],
-            dst_ref=tile.at[k, 0, pl.ds(1, experts - 1)],
+            src_ref=outgoing.at[k, others],
+            dst_ref=tile.at[k, 0, others],
             send_sem=z_send.at[k], recv_sem=z_recv.at[k],
             device_id={"loop": along(1)}, device_id_type=MESH,
         )
 
     def y_copy(k):
         return pltpu.make_async_remote_copy(
-            src_ref=tile.at[k, 0], dst_ref=tile.at[k, 1],
+            src_ref=tile.at[k, 0, others], dst_ref=tile.at[k, 1, others],
             send_sem=y_send.at[k], recv_sem=y_recv.at[k],
+            device_id={"loop": side}, device_id_type=MESH,
+        )
+
+    def y_own():
+        return pltpu.make_async_remote_copy(
+            src_ref=tile.at[:, 0, 0], dst_ref=tile.at[:, 1, 0],
+            send_sem=y_send.at[chunks], recv_sem=y_recv.at[chunks],
             device_id={"loop": side}, device_id_type=MESH,
         )
 
@@ -111,16 +124,16 @@
     for k in range(chunks):
         low = tokens[:, k * span:k * span + width]
         high = tokens[:, k * span + width:(k + 1) * span]
-        picked = lax.dot_general(
-            pick, jnp.concatenate([low, high], axis=0), (((0,), (0,)), ((), ())),
-            preferred_element_type=jnp.float32,
+        picked = jnp.dot(
+            pick, jnp.concatenate([low, high], axis=0), preferred_element_type=jnp.float32
         ).astype(jnp.bfloat16).reshape(experts, block, width)
         outgoing[k] = picked
         tile[k, 0, 0] = picked[0]
         if k == 0:
             pl.semaphore_wait(barrier, experts + 1)
-        for d in range(1, experts):
-            z_copy(k, d).start()
+        if k < AHEAD:
+            z_start(k)
+    y_own().start()
 
     def gate_up(k):
         arrived = tile[k].astype(jnp.float32).reshape(SLICES * experts, block, width)
@@ -143,6 +156,10 @@
         if t < chunks:
             z_all(t).wait_recv()
             y_copy(t).start()
+            if t + AHEAD < chunks:
+                z_start(t + AHEAD)
+        if t == 1:
+            y_own().wait_recv()
         if 0 <= t - 1 < chunks:
             y_copy(t - 1).wait_recv()
             c_copy(t - 1).start()
@@ -163,8 +180,15 @@
 
     def yb_copy(k):
         return pltpu.make_async_remote_copy(
-            src_ref=side_out.at[k], dst_ref=side_in.at[k],
+            src_ref=side_out.at[k, others], dst_ref=side_in.at[k, others],
             send_sem=yb_send.at[k], recv_sem=yb_recv.at[k],
+            device_id={"loop": side}, device_id_type=MESH,
+        )
+
+    def yb_own():
+        return pltpu.make_async_remote_copy(
+            src_ref=side_out.at[:, 0], dst_ref=side_in.at[:, 0],
+            send_sem=yb_send.at[chunks], recv_sem=yb_recv.at[chunks],
             device_id={"loop": side}, device_id_type=MESH,
         )
 
@@ -177,13 +201,13 @@
 
     def zb_all(k):
         return pltpu.make_async_remote_copy(
-            src_ref=back_out.at[k, pl.ds(1, experts - 1)],
-            dst_ref=back_in.at[k, pl.ds(1, experts - 1)],
+            src_ref=back_out.at[k, others],
+            dst_ref=back_in.at[k, others],
             send_sem=zb_send.at[k], recv_sem=zb_recv.at[k],
             device_id={"loop": along(1)}, device_id_type=MESH,
         )
 
-    scaled = jnp.concatenate([select_low * scale, select_high * scale], axis=0)
+    scaled = jnp.concatenate([select_low * scale, select_high * scale], axis=1).T
     coarse = scaled.astype(jnp.bfloat16)
     fine = (scaled - coarse.astype(jnp.float32)).astype(jnp.bfloat16)
     mixing = jnp.concatenate([coarse, fine], axis=0)
@@ -204,18 +228,23 @@
     def core_sum(k):
         cb_copy(k).wait_recv()
         side_out[k] = (own_part[k, 1] + core_in[k, 1].astype(jnp.float32)).astype(jnp.bfloat16)
-        yb_copy(k).start()
+        if k < AHEAD:
+            yb_copy(k).start()
         own_part[k, 0] = own_part[k, 0] + core_in[k, 0].astype(jnp.float32)
 
     def side_sum(k):
         yb_copy(k).wait_recv()
-        total = (own_part[k, 0] + side_in[k].astype(jnp.float32)).astype(jnp.bfloat16)
-        back_out[k] = total
+        if k + AHEAD < chunks:
+            yb_copy(k + AHEAD).start()
+        if k == max(0, chunks - 1 - AHEAD):
+            yb_own().start()
+        total = own_part[k, 0, 1:] + side_in[k, 1:].astype(jnp.float32)
+        back_out[k, 1:] = total.astype(jnp.bfloat16)
         for d in range(1, experts):
             zb_copy(k, d).start()
-        back_in[k, 0] = total[0]
 
     def mix(k):
+        back_in[k, 0] = (own_part[k, 0, 0] + side_in[k, 0].astype(jnp.float32)).astype(jnp.bfloat16)
         zb_all(k).wait_recv()
         m = jnp.dot(
             mixing, back_in[k].reshape(columns, width), preferred_element_type=jnp.float32
@@ -229,12 +258,14 @@
             down(t)
         if t >= 1:
             core_sum(t - 1)
-    for t in range(chunks + 1):
-        if t < chunks:
-            side_sum(t)
-        if t >= 1:
-            mix(t - 1)
-
+    for k in range(chunks):
+        side_sum(k)
+    yb_own().wait_recv()
+    for k in range(chunks):
+        mix(k)
+
+    y_own().wait_send()
+    yb_own().wait_send()
     for k in range(chunks):
         z_all(k).wait_send()
         y_copy(k).wait_send()
@@ -277,7 +308,7 @@
             pltpu.VMEM((chunks, experts, block, width), bf16),
             pltpu.VMEM((chunks, experts, block, width), bf16),
             dma((3, chunks)),
-        ] + [dma((chunks,)) for _ in range(12)],
+        ] + [dma((chunks + 1,)) for _ in range(12)],
         compiler_params=pltpu.CompilerParams(
             collective_id=0, has_side_effects=True, vmem_limit_bytes=56 * 1024 * 1024
         ),
@@ -286,7 +317,7 @@
             bytes_accessed=6 * model_width * units,
             transcendentals=rows * units,
         ),
-    )(tokens, expert_ids, keep_mask, route_weight, gate_weight, up_weight, down_weight)
+    )(tokens, expert_ids.T, keep_mask.T, route_weight.T, gate_weight, up_weight, down_weight)
 
 
 def solution(mesh):

time: 43.8 us -> 35.1 us (0.80)
  Pallas kernels: 37.5 us -> 33 us
  local copies, waits for them, and re-layouts: 6 us -> 1.87 us
    pallas_call x1, Pallas kernels: 37.5 us -> 33 us  [local(): pl.pallas_call(functools.partial(kernel, experts), out_shape=jax.ShapeDty...]
    unnamed x4 -> x1, local copies, waits for them, and re-layouts: 6 us -> 1.87 us
where the time goes in v2:
time: 35.1 us; the launch traced here: 34.9 us
  Pallas kernels  33 us (94%)
  local copies, waits for them, and re-layouts  1.87 us (5%)
    pallas_call x1, Pallas kernels, local(): pl.pallas_call(functools.partial(kernel, experts), out_shape=jax.ShapeDty...  33 us
    unnamed x1, local copies, waits for them, and re-layouts  1.87 us

profile of v2, /device:TPU:0, one launch (start us, length us, event | category | flops | bytes accessed | tf_op | source)
XLA Modules:
  0.0 34.9 jit_solution(16577999925717645813)
XLA Ops:
  0.0 33.0 %shard_map.73 = bf16[64,4096]{1,0:T(8,128)(2,1)} custom-call(bf16[64,4096]{1,0:T(8,128)(2,1)} %tokens.1, s32[8,64]{1,0:T(8,128)} %bitcast.3, s32[8,64]{1,0:T(8,128)} %bitcast.4, f32[8,64]{1,0:T(8,128)} %bitcast.5, bf16[1,4096,384]{2,1,0:T(8,128)(2,1)} %gate_hbm.1, bf16[1,4096,384]{2,1,0:T(8,128)(2,1)} %up_hbm.1, bf16[1,384,4096]{2,1,0:T(8,128)(2,1)} %down_hbm.1), custom_call_target="tpu_custom_call" | custom-call | flops 1207959552 | bytes 9437184 | tf_op jit(solution)/shard_map/pallas_call | solution.py:290
  33.1 1.9 %copy.9 = bf16[64,4096]{1,0:T(8,128)(2,1)} copy(bf16[64,4096]{1,0:T(8,128)(2,1)} %shard_map.73) | data formatting | bytes 1048576

commit v3 on v2

--- a/solution.py
+++ b/solution.py
@@ -9,7 +9,7 @@
 
 SLICES = 4
 SEND = 8
-CHUNKS = 2
+CHUNKS = 4
 AHEAD = 2
 MESH = pl.DeviceIdType.MESH
 
@@ -19,9 +19,9 @@
     tokens, ids, keep, route, gate_hbm, up_hbm, down_hbm,
     out,
     outgoing, tile, gate_w, up_w, down_w, gate_acc, up_acc, own_part,
-    core_out, core_in, side_out, side_in, back_out, back_in,
-    weight_sem, z_send, z_recv, y_send, y_recv, c_send, c_recv,
-    cb_send, cb_recv, yb_send, yb_recv, zb_send, zb_recv,
+    side_out, side_in, back_out, back_in,
+    weight_sem, push_send, push_recv, z_send, z_recv, y_send, y_recv,
+    yb_send, yb_recv, zb_send, zb_recv,
 ):
     place = lax.axis_index("loop")
     mine = lax.div(place, SLICES)
@@ -37,7 +37,7 @@
     span = 2 * width
     block = 2 * SEND
     columns = experts * block
-    rows = SLICES * experts * SEND
+    rows = 2 * experts * SEND
     others = pl.ds(1, experts - 1)
 
     barrier = pltpu.get_barrier_semaphore()
@@ -50,12 +50,12 @@
     for k in range(chunks):
         at = pl.ds(k * span, span)
         loads.append((
-            pltpu.make_async_copy(gate_hbm.at[0, at], gate_w.at[at], weight_sem.at[0, k]),
-            pltpu.make_async_copy(up_hbm.at[0, at], up_w.at[at], weight_sem.at[1, k]),
+            pltpu.make_async_copy(gate_hbm.at[0, at], gate_w.at[0, at], weight_sem.at[0, k]),
+            pltpu.make_async_copy(up_hbm.at[0, at], up_w.at[0, at], weight_sem.at[1, k]),
         ))
         for load in loads[-1]:
             load.start()
-    down_load = pltpu.make_async_copy(down_hbm.at[0], down_w, weight_sem.at[2, 0])
+    down_load = pltpu.make_async_copy(down_hbm.at[0], down_w.at[0], weight_sem.at[2, 0])
     down_load.start()
 
     row_count = tokens.shape[0]
@@ -114,10 +114,16 @@
             device_id={"loop": side}, device_id_type=MESH,
         )
 
-    def c_copy(k):
-        return pltpu.make_async_remote_copy(
-            src_ref=tile.at[k, pl.ds(0, 2)], dst_ref=tile.at[k, pl.ds(2, 2)],
-            send_sem=c_send.at[k], recv_sem=c_recv.at[k],
+    def push(which, k):
+        at = pl.ds(k * span, span)
+        source, target = (
+            (gate_hbm.at[0, at], gate_w.at[1, at]),
+            (up_hbm.at[0, at], up_w.at[1, at]),
+            (down_hbm.at[0, :, at], down_w.at[1, :, at]),
+        )[which]
+        return pltpu.make_async_remote_copy(
+            src_ref=source, dst_ref=target,
+            send_sem=push_send.at[which, k], recv_sem=push_recv.at[which, k],
             device_id={"loop": core}, device_id_type=MESH,
         )
 
@@ -133,26 +139,42 @@
             pl.semaphore_wait(barrier, experts + 1)
         if k < AHEAD:
             z_start(k)
+        if k == 0:
+            for i in range(chunks):
+                push(0, i).start()
+                push(1, i).start()
+            for i in range(chunks):
+                push(2, i).start()
     y_own().start()
 
+    scaled = jnp.concatenate([select_low * scale, select_high * scale], axis=1).T
+    coarse = scaled.astype(jnp.bfloat16)
+    fine = (scaled - coarse.astype(jnp.float32)).astype(jnp.bfloat16)
+    mixing = jnp.concatenate([coarse, fine], axis=0)
+
     def gate_up(k):
-        arrived = tile[k].astype(jnp.float32).reshape(SLICES * experts, block, width)
+        arrived = tile[k].astype(jnp.float32).reshape(2 * experts, block, width)
         x = jnp.concatenate(
             [arrived[:, :SEND].reshape(rows, width), arrived[:, SEND:].reshape(rows, width)], axis=1
         ).astype(jnp.bfloat16)
-        for load in loads[k]:
-            load.wait()
         at = pl.ds(k * span, span)
-        gate = jnp.dot(x, gate_w[at], preferred_element_type=jnp.float32)
-        up = jnp.dot(x, up_w[at], preferred_element_type=jnp.float32)
-        if k == 0:
-            gate_acc[...] = gate
-            up_acc[...] = up
-        else:
-            gate_acc[...] += gate
-            up_acc[...] += up
-
-    for t in range(chunks + 2):
+        for j in range(2):
+            if j == 0:
+                for load in loads[k]:
+                    load.wait()
+            else:
+                push(0, k).wait_recv()
+                push(1, k).wait_recv()
+            gate = jnp.dot(x, gate_w[j, at], preferred_element_type=jnp.float32)
+            up = jnp.dot(x, up_w[j, at], preferred_element_type=jnp.float32)
+            if k == 0:
+                gate_acc[j] = gate
+                up_acc[j] = up
+            else:
+                gate_acc[j] += gate
+                up_acc[j] += up
+
+    for t in range(chunks + 1):
         if t < chunks:
             z_all(t).wait_recv()
             y_copy(t).start()
@@ -160,23 +182,13 @@
                 z_start(t + AHEAD)
         if t == 1:
             y_own().wait_recv()
-        if 0 <= t - 1 < chunks:
+        if t >= 1:
             y_copy(t - 1).wait_recv()
-            c_copy(t - 1).start()
-        if 0 <= t - 2 < chunks:
-            c_copy(t - 2).wait_recv()
-            gate_up(t - 2)
+            gate_up(t - 1)
 
     gate = gate_acc[...]
     hidden = (gate / (1.0 + jnp.exp(-gate)) * up_acc[...]).astype(jnp.bfloat16)
     down_load.wait()
-
-    def cb_copy(k):
-        return pltpu.make_async_remote_copy(
-            src_ref=core_out.at[k], dst_ref=core_in.at[k],
-            send_sem=cb_send.at[k], recv_sem=cb_recv.at[k],
-            device_id={"loop": core}, device_id_type=MESH,
-        )
 
     def yb_copy(k):
         return pltpu.make_async_remote_copy(
@@ -207,30 +219,22 @@
             device_id={"loop": along(1)}, device_id_type=MESH,
         )
 
-    scaled = jnp.concatenate([select_low * scale, select_high * scale], axis=1).T
-    coarse = scaled.astype(jnp.bfloat16)
-    fine = (scaled - coarse.astype(jnp.float32)).astype(jnp.bfloat16)
-    mixing = jnp.concatenate([coarse, fine], axis=0)
-
     def down(k):
-        y = jnp.dot(hidden, down_w[:, k * span:(k + 1) * span], preferred_element_type=jnp.float32)
+        push(2, k).wait_recv()
+        at = pl.ds(k * span, span)
+        y = jnp.dot(hidden[0], down_w[0, :, at], preferred_element_type=jnp.float32)
+        y += jnp.dot(hidden[1], down_w[1, :, at], preferred_element_type=jnp.float32)
         y = jnp.concatenate(
             [
-                y[:, :width].reshape(SLICES * experts, SEND, width),
-                y[:, width:].reshape(SLICES * experts, SEND, width),
+                y[:, :width].reshape(2 * experts, SEND, width),
+                y[:, width:].reshape(2 * experts, SEND, width),
             ],
             axis=1,
-        ).reshape(SLICES, experts, block, width)
-        core_out[k] = y[2:].astype(jnp.bfloat16)
-        cb_copy(k).start()
-        own_part[k] = y[:2]
-
-    def core_sum(k):
-        cb_copy(k).wait_recv()
-        side_out[k] = (own_part[k, 1] + core_in[k, 1].astype(jnp.float32)).astype(jnp.bfloat16)
+        ).reshape(2, experts, block, width)
+        side_out[k] = y[1].astype(jnp.bfloat16)
         if k < AHEAD:
             yb_copy(k).start()
-        own_part[k, 0] = own_part[k, 0] + core_in[k, 0].astype(jnp.float32)
+        own_part[k] = y[0]
 
     def side_sum(k):
         yb_copy(k).wait_recv()
@@ -238,13 +242,13 @@
             yb_copy(k + AHEAD).start()
         if k == max(0, chunks - 1 - AHEAD):
             yb_own().start()
-        total = own_part[k, 0, 1:] + side_in[k, 1:].astype(jnp.float32)
+        total = own_part[k, 1:] + side_in[k, 1:].astype(jnp.float32)
         back_out[k, 1:] = total.astype(jnp.bfloat16)
         for d in range(1, experts):
             zb_copy(k, d).start()
 
     def mix(k):
-        back_in[k, 0] = (own_part[k, 0, 0] + side_in[k, 0].astype(jnp.float32)).astype(jnp.bfloat16)
+        back_in[k, 0] = (own_part[k, 0] + side_in[k, 0].astype(jnp.float32)).astype(jnp.bfloat16)
         zb_all(k).wait_recv()
         m = jnp.dot(
             mixing, back_in[k].reshape(columns, width), preferred_element_type=jnp.float32
@@ -253,11 +257,8 @@
         out[:, k * span:k * span + width] = m[:row_count].astype(jnp.bfloat16)
         out[:, k * span + width:(k + 1) * span] = m[row_count:].astype(jnp.bfloat16)
 
-    for t in range(chunks + 1):
-        if t < chunks:
-            down(t)
-        if t >= 1:
-            core_sum(t - 1)
+    for k in range(chunks):
+        down(k)
     for k in range(chunks):
         side_sum(k)
     yb_own().wait_recv()
@@ -269,8 +270,8 @@
     for k in range(chunks):
         z_all(k).wait_send()
         y_copy(k).wait_send()
-        c_copy(k).wait_send()
-        cb_copy(k).wait_send()
+        for i in range(3):
+            push(i, k).wait_send()
         yb_copy(k).wait_send()
         zb_all(k).wait_send()
 
@@ -282,7 +283,7 @@
     chunks = CHUNKS
     width = model_width // (2 * chunks)
     block = 2 * SEND
-    rows = SLICES * experts * SEND
+    rows = 2 * experts * SEND
     bf16, f32 = jnp.bfloat16, jnp.float32
     vmem = pl.BlockSpec(memory_space=pltpu.VMEM)
     hbm = pl.BlockSpec(memory_space=pl.ANY)
@@ -294,28 +295,28 @@
         out_specs=vmem,
         scratch_shapes=[
             pltpu.VMEM((chunks, experts, block, width), bf16),
-            pltpu.VMEM((chunks, SLICES, experts, block, width), bf16),
-            pltpu.VMEM((model_width, units), bf16),
-            pltpu.VMEM((model_width, units), bf16),
-            pltpu.VMEM((units, model_width), bf16),
-            pltpu.VMEM((rows, units), f32),
-            pltpu.VMEM((rows, units), f32),
-            pltpu.VMEM((chunks, 2, experts, block, width), f32),
             pltpu.VMEM((chunks, 2, experts, block, width), bf16),
-            pltpu.VMEM((chunks, 2, experts, block, width), bf16),
+            pltpu.VMEM((2, model_width, units), bf16),
+            pltpu.VMEM((2, model_width, units), bf16),
+            pltpu.VMEM((2, units, model_width), bf16),
+            pltpu.VMEM((2, rows, units), f32),
+            pltpu.VMEM((2, rows, units), f32),
+            pltpu.VMEM((chunks, experts, block, width), f32),
             pltpu.VMEM((chunks, experts, block, width), bf16),
             pltpu.VMEM((chunks, experts, block, width), bf16),
             pltpu.VMEM((chunks, experts, block, width), bf16),
             pltpu.VMEM((chunks, experts, block, width), bf16),
             dma((3, chunks)),
-        ] + [dma((chunks + 1,)) for _ in range(12)],
+            dma((3, chunks)),
+            dma((3, chunks)),
+        ] + [dma((chunks + 1,)) for _ in range(8)],
         compiler_params=pltpu.CompilerParams(
             collective_id=0, has_side_effects=True, vmem_limit_bytes=56 * 1024 * 1024
         ),
         cost_estimate=pl.CostEstimate(
-            flops=6 * rows * model_width * units,
+            flops=12 * rows * model_width * units,
             bytes_accessed=6 * model_width * units,
-            transcendentals=rows * units,
+            transcendentals=2 * rows * units,
         ),
     )(tokens, expert_ids.T, keep_mask.T, route_weight.T, gate_weight, up_weight, down_weight)
 

time: 35.1 us -> 33.1 us (0.943)
  Pallas kernels: 33 us -> 31 us
    pallas_call x1, Pallas kernels: 33 us -> 31 us  [local(): pl.pallas_call(functools.partial(kernel, experts), out_shape=jax.ShapeDty...]
where the time goes in v3:
time: 33.1 us; the launch traced here: 32.9 us
  Pallas kernels  31 us (94%)
  local copies, waits for them, and re-layouts  1.87 us (6%)
    pallas_call x1, Pallas kernels, local(): pl.pallas_call(functools.partial(kernel, experts), out_shape=jax.ShapeDty...  31 us
    unnamed x1, local copies, waits for them, and re-layouts  1.87 us

profile of v3, /device:TPU:0, one launch (start us, length us, event | category | flops | bytes accessed | tf_op | source)
XLA Modules:
  0.0 32.9 jit_solution(11754260055941238485)
XLA Ops:
  0.0 31.0 %shard_map.73 = bf16[64,4096]{1,0:T(8,128)(2,1)} custom-call(bf16[64,4096]{1,0:T(8,128)(2,1)} %tokens.1, s32[8,64]{1,0:T(8,128)} %bitcast.3, s32[8,64]{1,0:T(8,128)} %bitcast.4, f32[8,64]{1,0:T(8,128)} %bitcast.5, bf16[1,4096,384]{2,1,0:T(8,128)(2,1)} %gate_hbm.1, bf16[1,4096,384]{2,1,0:T(8,128)(2,1)} %up_hbm.1, bf16[1,384,4096]{2,1,0:T(8,128)(2,1)} %down_hbm.1), custom_call_target="tpu_custom_call" | custom-call | flops 1207959552 | bytes 9437184 | tf_op jit(solution)/shard_map/pallas_call | solution.py:291
  31.0 1.9 %copy.9 = bf16[64,4096]{1,0:T(8,128)(2,1)} copy(bf16[64,4096]{1,0:T(8,128)(2,1)} %shard_map.73) | data formatting | bytes 1048576

commit v4 on v3

--- a/solution.py
+++ b/solution.py
@@ -11,15 +11,16 @@
 SEND = 8
 CHUNKS = 4
 AHEAD = 2
+AHEAD_BACK = 4
 MESH = pl.DeviceIdType.MESH
 
 
 def kernel(
     experts,
     tokens, ids, keep, route, gate_hbm, up_hbm, down_hbm,
-    out,
+    out_hbm,
     outgoing, tile, gate_w, up_w, down_w, gate_acc, up_acc, own_part,
-    side_out, side_in, back_out, back_in,
+    side_out, side_in, back_out, back_in, out, out_sem,
     weight_sem, push_send, push_recv, z_send, z_recv, y_send, y_recv,
     yb_send, yb_recv, zb_send, zb_recv,
 ):
@@ -232,21 +233,25 @@
             axis=1,
         ).reshape(2, experts, block, width)
         side_out[k] = y[1].astype(jnp.bfloat16)
-        if k < AHEAD:
+        if k < AHEAD_BACK:
             yb_copy(k).start()
         own_part[k] = y[0]
 
     def side_sum(k):
         yb_copy(k).wait_recv()
-        if k + AHEAD < chunks:
-            yb_copy(k + AHEAD).start()
-        if k == max(0, chunks - 1 - AHEAD):
+        if k + AHEAD_BACK < chunks:
+            yb_copy(k + AHEAD_BACK).start()
+        if k == max(0, chunks - 1 - AHEAD_BACK):
             yb_own().start()
         total = own_part[k, 1:] + side_in[k, 1:].astype(jnp.float32)
         back_out[k, 1:] = total.astype(jnp.bfloat16)
         for d in range(1, experts):
             zb_copy(k, d).start()
 
+    def store(k):
+        at = pl.ds(k * span, span)
+        return pltpu.make_async_copy(out.at[:, at], out_hbm.at[:, at], out_sem.at[k])
+
     def mix(k):
         back_in[k, 0] = (own_part[k, 0] + side_in[k, 0].astype(jnp.float32)).astype(jnp.bfloat16)
         zb_all(k).wait_recv()
@@ -264,6 +269,7 @@
     yb_own().wait_recv()
     for k in range(chunks):
         mix(k)
+        store(k).start()
 
     y_own().wait_send()
     yb_own().wait_send()
@@ -272,6 +278,7 @@
         y_copy(k).wait_send()
         for i in range(3):
             push(i, k).wait_send()
+        store(k).wait()
         yb_copy(k).wait_send()
         zb_all(k).wait_send()
 
@@ -292,7 +299,7 @@
         functools.partial(kernel, experts),
         out_shape=jax.ShapeDtypeStruct((row_count, model_width), bf16),
         in_specs=[vmem, vmem, vmem, vmem, hbm, hbm, hbm],
-        out_specs=vmem,
+        out_specs=hbm,
         scratch_shapes=[
             pltpu.VMEM((chunks, experts, block, width), bf16),
             pltpu.VMEM((chunks, 2, experts, block, width), bf16),
@@ -306,6 +313,8 @@
             pltpu.VMEM((chunks, experts, block, width), bf16),
             pltpu.VMEM((chunks, experts, block, width), bf16),
             pltpu.VMEM((chunks, experts, block, width), bf16),
+            pltpu.VMEM((row_count, model_width), bf16),
+            dma((chunks,)),
             dma((3, chunks)),
             dma((3, chunks)),
             dma((3, chunks)),

time: 33.1 us -> 32.6 us (0.985)
  Pallas kernels: 31 us -> 30.6 us
    pallas_call x1, Pallas kernels: 31 us -> 30.6 us  [local(): pl.pallas_call(functools.partial(kernel, experts), out_shape=jax.ShapeDty...]
where the time goes in v4:
time: 32.6 us; the launch traced here: 32.5 us
  Pallas kernels  30.6 us (94%)
  local copies, waits for them, and re-layouts  1.87 us (6%)
    pallas_call x1, Pallas kernels, local(): pl.pallas_call(functools.partial(kernel, experts), out_shape=jax.ShapeDty...  30.6 us
    unnamed x1, local copies, waits for them, and re-layouts  1.87 us

profile of v4, /device:TPU:0, one launch (start us, length us, event | category | flops | bytes accessed | tf_op | source)
XLA Modules:
  0.0 32.5 jit_solution(8818407524731634421)
XLA Ops:
  0.0 30.6 %shard_map.73 = bf16[64,4096]{1,0:T(8,128)(2,1)} custom-call(bf16[64,4096]{1,0:T(8,128)(2,1)} %tokens.1, s32[8,64]{1,0:T(8,128)} %bitcast.3, s32[8,64]{1,0:T(8,128)} %bitcast.4, f32[8,64]{1,0:T(8,128)} %bitcast.5, bf16[1,4096,384]{2,1,0:T(8,128)(2,1)} %gate_hbm.1, bf16[1,4096,384]{2,1,0:T(8,128)(2,1)} %up_hbm.1, bf16[1,384,4096]{2,1,0:T(8,128)(2,1)} %down_hbm.1), custom_call_target="tpu_custom_call" | custom-call | flops 1207959552 | bytes 9437184 | tf_op jit(solution)/shard_map/pallas_call | solution.py:298
  30.6 1.9 %copy.9 = bf16[64,4096]{1,0:T(8,128)(2,1)} copy(bf16[64,4096]{1,0:T(8,128)(2,1)} %shard_map.73) | data formatting | bytes 1048576
